TPU v7x, 512 devices: a whole 4x4x16 slice. The times are simulated.
512 devices in a mesh: mesh: 32 (over z, core), run: 16 (over y, x).
Axes of the slice: x: 4, y: 4, z: 16, core: 2. Of those that a mesh axis runs over, the one named last changes fastest.
Arguments:
- snapshots: bfloat16 [65536, 2048], P('mesh', 'run'), may hold values from -6 to 6
- block_cols: int32 [1024, 16], P('mesh'), may hold values from 0 to 1023, as said below
- mass_blocks: bfloat16 [1024, 64, 1024], P('mesh'), as said below
Outputs:
- gram: float32 [2048, 2048], P('mesh', 'run')
Inputs may be any that keep to these rules, and one draw needn't show every extreme that they name: `block_cols`: block row b names 16 different block columns, the first of them b itself; all lie from 2 blocks before the first block row of shard b // 32 to 2 blocks after its last. In every shard but the first, its first block row names the block 2 before the shard; in every shard but the last, its last block row names the block 2 after it. `mass_blocks`: entry [b, i, k * 64 + j] is row i, column j of the k-th stored block of block row b, in the order of block_cols.
All inputs are finite; a program needn't handle non-finite values.
Results may differ from a plain program's by a relative error of at most 0.00056.
Values may be sent and summed in bfloat16 or wider, within the bound.
A program may use at most 64 MiB of HBM per device.

v0:
```python
import jax
import jax.numpy as jnp
from jax import lax
from jax.sharding import PartitionSpec as P

BLK = 64
HB = 2


def extended(block, sides, width):
    for axis, dim in sides:
        count = lax.axis_size(axis)
        forward = [(i, i + 1) for i in range(count - 1)]
        backward = [(target, source) for source, target in forward]
        low = lax.ppermute(
            lax.slice_in_dim(block, block.shape[dim] - width, None, axis=dim), axis, forward
        )
        high = lax.ppermute(lax.slice_in_dim(block, 0, width, axis=dim), axis, backward)
        block = jnp.concatenate([low, block, high], axis=dim)
    return block


def contract_nodes(left_cols, right_cols):
    return lax.dot_general(
        left_cols, right_cols, (((0,), (0,)), ((), ())), preferred_element_type=jnp.float32
    )


def on_device(snapshots, block_cols, mass_blocks):
    node_count = snapshots.shape[0]
    column_count = snapshots.shape[1]
    blocks_here = node_count // BLK
    stored_count = block_cols.shape[1]
    rim_width = HB * BLK
    padded = extended(snapshots, (("mesh", 0),), rim_width)
    shard_index = lax.axis_index("mesh")
    local_cols = block_cols - (shard_index * blocks_here - HB)
    blocked = padded.reshape(blocks_here + 2 * HB, BLK, column_count)
    picked = blocked[local_cols].reshape(blocks_here, stored_count * BLK, column_count)
    weighted = jnp.einsum("bim,bmc->bic", mass_blocks, picked, preferred_element_type=jnp.float32)
    weighted = weighted.astype(jnp.bfloat16).reshape(node_count, column_count)
    gathered = lax.all_gather(snapshots, "run", axis=1, tiled=True)
    partial_term = contract_nodes(gathered, weighted)
    gram = lax.psum_scatter(partial_term, "mesh", scatter_dimension=0, tiled=True)
    return gram


def solution(mesh):
    placed = (P("mesh", "run"), P("mesh", None), P("mesh", None, None))
    return jax.shard_map(
        on_device, mesh=mesh, in_specs=placed, out_specs=P("mesh", "run"), check_vma=False
    )
```

profile of v0, /device:TPU:2, one launch (start us, length us, event | category | flops | bytes accessed | tf_op | source)
XLA Modules:
  0.0 229.1 jit_solution(6387576160055392372)
XLA Ops:
  6.5 0.0 all-gather.2.cloned.1.call-start
  6.5 0.7 all-gather.2.cloned.1.call-update
  7.3 0.0 reduce-scatter.4.cloned.1.call-start
  7.3 0.8 fusion
  8.1 1.7 collective-permute-start
  9.8 1.3 collective-permute-start.1
  11.1 0.7 compare_select_fusion
  11.8 0.1 copy.7
  11.9 0.1 reshape.14
  12.0 0.0 collective-permute-done
  12.0 2.6 %collective-permute-done.1 = bf16[128,128]{1,0:T(8,128)(2,1)S(1)} collective-permute-done((bf16[128,128]{1,0:T(8,128)(2,1)S(1)}, bf16[128,128]{1,0:T(8,128)(2,1)S(1)}, u32[]{:S(2)}, u32[]{:S(2)}) %collective-permute-start.1) | collective-permute-done | bytes 32800 | tf_op jit(solution)/shard_map/ppermute | solution.py:18
  14.6 1.1 pad_maximum_fusion
  15.7 13.4 %gather_fusion = bf16[512,64,128]{2,1,0:T(8,128)(2,1)} fusion(bf16[36,64,128]{2,1,0:T(8,128)(2,1)S(1)} %bitcast.12, s32[1024]{0:T(1024)S(1)} %pad_clamp_fusion), kind=kCustom, calls=%fused_computation | custom fusion | bytes 16779264 | tf_op jit(solution)/shard_map/gather | solution.py:39
  29.1 6.6 %convolution_convert_fusion = bf16[32,128,64]{1,2,0:T(8,128)(2,1)S(1)} fusion(bf16[32,64,1024]{2,1,0:T(8,128)(2,1)} %param.5, bf16[32,1024,128]{2,1,0:T(8,128)(2,1)} %bitcast.13), kind=kOutput, calls=%fused_computation.2 | convolution fusion | flops 537133056 | bytes 13107200 | tf_op jit(solution)/shard_map/bim,bmc->bic/dot_general | solution.py:40
  35.8 72.4 %all-gather.2.cloned.1.call-done = bf16[2048,2048]{1,0:T(8,128)(2,1)} async-done(((bf16[2048,128]{1,0:T(8,128)(2,1)}), bf16[2048,2048]{1,0:T(8,128)(2,1)}) %all-gather.2.cloned.1.call-update) | async-done | bytes 8388624 | tf_op jit(solution)/shard_map/all_gather | solution.py:42
  108.2 4.7 %convolution_bitcast_fusion = f32[2048,128]{0,1:T(8,128)S(1)} fusion(bf16[2048,128]{1,0:T(8,128)(2,1)S(1)} %bitcast.14, bf16[2048,2048]{1,0:T(8,128)(2,1)} %all-gather.2.cloned.1.call-done), kind=kOutput, calls=%fused_computation.1 | convolution fusion | flops 1073741824 | bytes 9961472 | tf_op jit(solution)/shard_map/dot_general | solution.py:24
  112.9 1.3 copy.9
  114.2 0.0 reduce-scatter.4.cloned.1.call-update
  114.2 108.1 %reduce-scatter.4.cloned.1.call-done = f32[64,128]{1,0:T(8,128)} async-done(((f32[2048,128]{1,0:T(8,128)}), f32[64,128]{1,0:T(8,128)}) %reduce-scatter.4.cloned.1.call-update) | async-done | bytes 32784 | tf_op jit(solution)/shard_map/reduce_scatter | solution.py:44
  (1 shorter events, 0.0 us)
Async XLA Ops:
  6.5 101.7 %all-gather.2.cloned.1.call-start = ((), (), s32[]{:S(2)}) async-start(), calls=%async_computation.1 | async-start | bytes 8912896 | tf_op jit(solution)/shard_map/all_gather | solution.py:42
  7.3 215.0 %reduce-scatter.4.cloned.1.call-start = ((), (), s32[]{:S(2)}) async-start(), calls=%async_computation.2 | async-start | bytes 1081344 | tf_op jit(solution)/shard_map/reduce_scatter | solution.py:44
  8.1 3.9 %collective-permute-start = (bf16[128,128]{1,0:T(8,128)(2,1)S(1)}, bf16[128,128]{1,0:T(8,128)(2,1)S(1)}, u32[]{:S(2)}, u32[]{:S(2)}) collective-permute-start(bf16[128,128]{1,0:T(8,128)(2,1)S(1)} %get-tuple-element.5), channel_id=1, source_target_pairs={{0,16},{16,32},{32,48},{48,64},{64,80},{80,96},{96,112},{112,128},... | collective-permute-start | bytes 98312 | tf_op jit(solution)/shard_map/ppermute | solution.py:15
  9.8 4.8 %collective-permute-start.1 = (bf16[128,128]{1,0:T(8,128)(2,1)S(1)}, bf16[128,128]{1,0:T(8,128)(2,1)S(1)}, u32[]{:S(2)}, u32[]{:S(2)}) collective-permute-start(bf16[128,128]{1,0:T(8,128)(2,1)S(1)} %get-tuple-element.6), channel_id=1, source_target_pairs={{16,0},{32,16},{48,32},{64,48},{80,64},{96,80},{112,96},{128,112},... | collective-permute-start | bytes 98312 | tf_op jit(solution)/shard_map/ppermute | solution.py:18
Sparse Core Ops, SparseCore 0:
  10.3 97.8 all-gather.1
  114.3 107.9 reduce-scatter.3
where the time goes:
time: 229 us
  waiting for transfers between devices  184 us (80%)
  local copies, waits for them, and re-layouts  15.7 us (7%)
  between operations  13.4 us (6%)
  matrix products  11.3 us (5%)
  starting transfers between devices  3.06 us (1%)
    reduce_scatter x1, waiting for transfers between devices, on_device(): lax.psum_scatter(partial_term, 'mesh', scatter_dimension=0, tiled=True)  108 us
    all_gather x1, waiting for transfers between devices, on_device(): gathered = lax.all_gather(snapshots, 'run', axis=1, tiled=True)  72.4 us
    gather x1, local copies, waits for them, and re-layouts, on_device(): blocked[local_cols].reshape(blocks_here, stored_count * BLK, column_count)  13.4 us
    dot_general x1, matrix products, on_device(): jnp.einsum('bim,bmc->bic', mass_blocks, picked, preferred_element_type=jn...  6.61 us
    dot_general x1, matrix products, contract_nodes(): lax.dot_general(left_cols, right_cols, (((0,), (0,)), ((), ())), preferre...  4.66 us
  transfers between devices with their start and end apart: 4, of which 3 were waited for; matrix products, arithmetic and copies ran while one was open for 10% of the time, Pallas kernels for 0%

commit v1 on v0

--- a/solution.py
+++ b/solution.py
@@ -5,6 +5,12 @@
 
 BLK = 64
 HB = 2
+
+
+def joined_along(tiles, dim):
+    tiles = jnp.moveaxis(tiles, 0, dim)
+    shape = tiles.shape
+    return tiles.reshape(*shape[:dim], shape[dim] * shape[dim + 1], *shape[dim + 2 :])
 
 
 def extended(block, sides, width):
@@ -39,7 +45,19 @@
     picked = blocked[local_cols].reshape(blocks_here, stored_count * BLK, column_count)
     weighted = jnp.einsum("bim,bmc->bic", mass_blocks, picked, preferred_element_type=jnp.float32)
     weighted = weighted.astype(jnp.bfloat16).reshape(node_count, column_count)
-    gathered = lax.all_gather(snapshots, "run", axis=1, tiled=True)
+    length = lax.axis_size("run")
+    pairs = [(i_2, (i_2 + 1) % length) for i_2 in range(length)]
+    back = [(b, a) for a, b in pairs]
+    lower, upper = ([], [])
+    for step in range(length - 1):
+        if step % 2 == 0:
+            lower.append(lax.ppermute(lower[-1] if lower else snapshots, "run", pairs))
+        else:
+            upper.append(lax.ppermute(upper[-1] if upper else snapshots, "run", back))
+    pieces = jnp.stack([*lower[::-1], snapshots, *upper])
+    shift = lax.axis_index("run") - len(lower)
+    pieces = pieces[(jnp.arange(length) - shift) % length]
+    gathered = joined_along(pieces, 1)
     partial_term = contract_nodes(gathered, weighted)
     gram = lax.psum_scatter(partial_term, "mesh", scatter_dimension=0, tiled=True)
     return gram

time: 229 us -> 313 us (1.37)
  starting transfers between devices: 3.06 us -> 67.4 us
  local copies, waits for them, and re-layouts: 15.7 us -> 53.5 us
  waiting for transfers between devices: 184 us -> 162 us
    all_gather x1 -> x0, waiting for transfers between devices: 72.4 us -> none  [on_device(): gathered = lax.all_gather(snapshots, 'run', axis=1, tiled=True)]
    ppermute x0 -> x15, starting transfers between devices: none -> 64.8 us  [the longest x7 39.5 us: on_device(): upper.append(lax.ppermute(upper[-1] if upper else snapshots, 'run', back))]
    ppermute x0 -> x15, waiting for transfers between devices: none -> 37.7 us  [the longest x8 35.2 us: on_device(): lower.append(lax.ppermute(lower[-1] if lower else snapshots, 'run', pairs))]
    unnamed x1 -> x25, local copies, waits for them, and re-layouts: 1.31 us -> 17.7 us
    reduce_scatter x1, waiting for transfers between devices: 108 us -> 124 us  [on_device(): lax.psum_scatter(partial_term, 'mesh', scatter_dimension=0, tiled=True)]
    transpose x0 -> x1, local copies, waits for them, and re-layouts: none -> 12.4 us  [joined_along(): tiles = jnp.moveaxis(tiles, 0, dim)]
    gather x0 -> x1, local copies, waits for them, and re-layouts: none -> 8.14 us  [on_device(): pieces = pieces[(jnp.arange(length) - shift) % length]]
  transfers between devices with their start and end apart: 4 -> 18, of which waited for: 3 -> 10; matrix products, arithmetic and copies ran while one was open for 10% -> 13% of each run, Pallas kernels for 0% -> 0%
where the time goes in v1:
time: 313 us; the launch traced here: 312 us
  waiting for transfers between devices  162 us (52%)
  starting transfers between devices  67.4 us (22%)
  local copies, waits for them, and re-layouts  53.5 us (17%)
  between operations  13.6 us (4%)
  matrix products  13 us (4%)
    reduce_scatter x1, waiting for transfers between devices, on_device(): lax.psum_scatter(partial_term, 'mesh', scatter_dimension=0, tiled=True)  124 us
    ppermute x7, starting transfers between devices, on_device(): upper.append(lax.ppermute(upper[-1] if upper else snapshots, 'run', back))  39.5 us
    ppermute x8, waiting for transfers between devices, on_device(): lower.append(lax.ppermute(lower[-1] if lower else snapshots, 'run', pairs))  35.2 us
    ppermute x8, starting transfers between devices, on_device(): lower.append(lax.ppermute(lower[-1] if lower else snapshots, 'run', pairs))  25.3 us
    unnamed x25, local copies, waits for them, and re-layouts  17.7 us
    gather x1, local copies, waits for them, and re-layouts, on_device(): blocked[local_cols].reshape(blocks_here, stored_count * BLK, column_count)  13.5 us
    transpose x1, local copies, waits for them, and re-layouts, joined_along(): tiles = jnp.moveaxis(tiles, 0, dim)  12.4 us
    gather x1, local copies, waits for them, and re-layouts, on_device(): pieces = pieces[(jnp.arange(length) - shift) % length]  8.14 us
  transfers between devices with their start and end apart: 18, of which 10 were waited for; matrix products, arithmetic and copies ran while one was open for 13% of the time, Pallas kernels for 0%

profile of v1, /device:TPU:2, one launch (start us, length us, event | category | flops | bytes accessed | tf_op | source)
XLA Modules:
  0.0 311.7 jit_solution(17677241988359092098)
XLA Ops:
  6.5 0.0 reduce-scatter.2.cloned.1.call-start
  6.5 3.4 %collective-permute-start = (bf16[2048,128]{1,0:T(8,128)(2,1)}, bf16[2048,128]{1,0:T(8,128)(2,1)S(1)}, u32[]{:S(2)}, u32[]{:S(2)}) collective-permute-start(bf16[2048,128]{1,0:T(8,128)(2,1)} %param.3), channel_id=1, source_target_pairs={{0,1},{1,2},{2,3},{3,4},{4,5},{5,6},{6,7},{7,8},{8,9},{9,10},{10,1... | collective-permute-start | bytes 1572872 | tf_op jit(solution)/shard_map/ppermute | solution.py:54
  9.9 12.4 %collective-permute-done = bf16[2048,128]{1,0:T(8,128)(2,1)S(1)} collective-permute-done((bf16[2048,128]{1,0:T(8,128)(2,1)}, bf16[2048,128]{1,0:T(8,128)(2,1)S(1)}, u32[]{:S(2)}, u32[]{:S(2)}) %collective-permute-start) | collective-permute-done | bytes 524320 | tf_op jit(solution)/shard_map/ppermute | solution.py:54
  22.3 3.4 %collective-permute-start.1 = (bf16[2048,128]{1,0:T(8,128)(2,1)S(1)}, bf16[2048,128]{1,0:T(8,128)(2,1)S(1)}, u32[]{:S(2)}, u32[]{:S(2)}) collective-permute-start(bf16[2048,128]{1,0:T(8,128)(2,1)S(1)} %collective-permute-done), channel_id=1, source_target_pairs={{0,1},{1,2},{2,3},{3,4},{4,5},{5,6},{6,7},{7,8},{8,9},{9,10},{10,1... | collective-permute-start | bytes 1572872 | tf_op jit(solution)/shard_map/ppermute | solution.py:54
  25.7 5.2 %collective-permute-start.8 = (bf16[2048,128]{1,0:T(8,128)(2,1)}, bf16[2048,128]{1,0:T(8,128)(2,1)S(1)}, u32[]{:S(2)}, u32[]{:S(2)}) collective-permute-start(bf16[2048,128]{1,0:T(8,128)(2,1)} %param.3), channel_id=1, source_target_pairs={{1,0},{2,1},{3,2},{4,3},{5,4},{6,5},{7,6},{8,7},{9,8},{10,9},{11,1... | collective-permute-start | bytes 1572872 | tf_op jit(solution)/shard_map/ppermute | solution.py:56
  30.9 5.2 %collective-permute-done.1 = bf16[2048,128]{1,0:T(8,128)(2,1)S(1)} collective-permute-done((bf16[2048,128]{1,0:T(8,128)(2,1)S(1)}, bf16[2048,128]{1,0:T(8,128)(2,1)S(1)}, u32[]{:S(2)}, u32[]{:S(2)}) %collective-permute-start.1) | collective-permute-done | bytes 524320 | tf_op jit(solution)/shard_map/ppermute | solution.py:54
  36.1 4.3 %collective-permute-start.2 = (bf16[2048,128]{1,0:T(8,128)(2,1)S(1)}, bf16[2048,128]{1,0:T(8,128)(2,1)S(1)}, u32[]{:S(2)}, u32[]{:S(2)}) collective-permute-start(bf16[2048,128]{1,0:T(8,128)(2,1)S(1)} %collective-permute-done.1), channel_id=1, source_target_pairs={{0,1},{1,2},{2,3},{3,4},{4,5},{5,6},{6,7},{7,8},{8,9},{9,10},{10,1... | collective-permute-start | bytes 1572872 | tf_op jit(solution)/shard_map/ppermute | solution.py:54
  40.4 0.0 collective-permute-done.8
  40.4 4.9 %collective-permute-start.9 = (bf16[2048,128]{1,0:T(8,128)(2,1)S(1)}, bf16[2048,128]{1,0:T(8,128)(2,1)S(1)}, u32[]{:S(2)}, u32[]{:S(2)}) collective-permute-start(bf16[2048,128]{1,0:T(8,128)(2,1)S(1)} %collective-permute-done.8), channel_id=1, source_target_pairs={{1,0},{2,1},{3,2},{4,3},{5,4},{6,5},{7,6},{8,7},{9,8},{10,9},{11,1... | collective-permute-start | bytes 1572872 | tf_op jit(solution)/shard_map/ppermute | solution.py:56
  45.3 5.2 %collective-permute-done.2 = bf16[2048,128]{1,0:T(8,128)(2,1)S(1)} collective-permute-done((bf16[2048,128]{1,0:T(8,128)(2,1)S(1)}, bf16[2048,128]{1,0:T(8,128)(2,1)S(1)}, u32[]{:S(2)}, u32[]{:S(2)}) %collective-permute-start.2) | collective-permute-done | bytes 524320 | tf_op jit(solution)/shard_map/ppermute | solution.py:54
  50.5 3.6 %collective-permute-start.3 = (bf16[2048,128]{1,0:T(8,128)(2,1)S(1)}, bf16[2048,128]{1,0:T(8,128)(2,1)S(1)}, u32[]{:S(2)}, u32[]{:S(2)}) collective-permute-start(bf16[2048,128]{1,0:T(8,128)(2,1)S(1)} %collective-permute-done.2), channel_id=1, source_target_pairs={{0,1},{1,2},{2,3},{3,4},{4,5},{5,6},{6,7},{7,8},{8,9},{9,10},{10,1... | collective-permute-start | bytes 1572872 | tf_op jit(solution)/shard_map/ppermute | solution.py:54
  54.1 1.3 collective-permute-done.9
  55.4 4.3 %collective-permute-start.10 = (bf16[2048,128]{1,0:T(8,128)(2,1)S(1)}, bf16[2048,128]{1,0:T(8,128)(2,1)S(1)}, u32[]{:S(2)}, u32[]{:S(2)}) collective-permute-start(bf16[2048,128]{1,0:T(8,128)(2,1)S(1)} %collective-permute-done.9), channel_id=1, source_target_pairs={{1,0},{2,1},{3,2},{4,3},{5,4},{6,5},{7,6},{8,7},{9,8},{10,9},{11,1... | collective-permute-start | bytes 1572872 | tf_op jit(solution)/shard_map/ppermute | solution.py:56
  59.7 5.2 %collective-permute-done.3 = bf16[2048,128]{1,0:T(8,128)(2,1)S(1)} collective-permute-done((bf16[2048,128]{1,0:T(8,128)(2,1)S(1)}, bf16[2048,128]{1,0:T(8,128)(2,1)S(1)}, u32[]{:S(2)}, u32[]{:S(2)}) %collective-permute-start.3) | collective-permute-done | bytes 524320 | tf_op jit(solution)/shard_map/ppermute | solution.py:54
  64.9 4.0 %collective-permute-start.4 = (bf16[2048,128]{1,0:T(8,128)(2,1)S(1)}, bf16[2048,128]{1,0:T(8,128)(2,1)}, u32[]{:S(2)}, u32[]{:S(2)}) collective-permute-start(bf16[2048,128]{1,0:T(8,128)(2,1)S(1)} %collective-permute-done.3), channel_id=1, source_target_pairs={{0,1},{1,2},{2,3},{3,4},{4,5},{5,6},{6,7},{7,8},{8,9},{9,10},{10,1... | collective-permute-start | bytes 1572872 | tf_op jit(solution)/shard_map/ppermute | solution.py:54
  68.9 1.2 collective-permute-done.10
  70.1 4.2 %collective-permute-start.11 = (bf16[2048,128]{1,0:T(8,128)(2,1)S(1)}, bf16[2048,128]{1,0:T(8,128)(2,1)}, u32[]{:S(2)}, u32[]{:S(2)}) collective-permute-start(bf16[2048,128]{1,0:T(8,128)(2,1)S(1)} %collective-permute-done.10), channel_id=1, source_target_pairs={{1,0},{2,1},{3,2},{4,3},{5,4},{6,5},{7,6},{8,7},{9,8},{10,9},{11,1... | collective-permute-start | bytes 1572872 | tf_op jit(solution)/shard_map/ppermute | solution.py:56
  74.4 5.8 %collective-permute-done.4 = bf16[2048,128]{1,0:T(8,128)(2,1)} collective-permute-done((bf16[2048,128]{1,0:T(8,128)(2,1)S(1)}, bf16[2048,128]{1,0:T(8,128)(2,1)}, u32[]{:S(2)}, u32[]{:S(2)}) %collective-permute-start.4) | collective-permute-done | bytes 524320 | tf_op jit(solution)/shard_map/ppermute | solution.py:54
  80.1 2.8 collective-permute-start.5
  82.9 0.8 fusion.2
  83.7 1.3 collective-permute-start.15
  85.0 1.3 collective-permute-start.16
  86.3 0.7 compare_select_fusion
  87.0 0.0 collective-permute-done.11
  87.0 6.7 %collective-permute-start.12 = (bf16[2048,128]{1,0:T(8,128)(2,1)}, bf16[2048,128]{1,0:T(8,128)(2,1)}, u32[]{:S(2)}, u32[]{:S(2)}) collective-permute-start(bf16[2048,128]{1,0:T(8,128)(2,1)} %collective-permute-done.11), channel_id=1, source_target_pairs={{1,0},{2,1},{3,2},{4,3},{5,4},{6,5},{7,6},{8,7},{9,8},{10,9},{11,1... | collective-permute-start | bytes 1572872 | tf_op jit(solution)/shard_map/ppermute | solution.py:56
  93.7 1.4 collective-permute-done.5
  95.1 1.9 collective-permute-start.6
  97.1 0.1 copy.6
  97.1 0.1 reshape.75
  97.2 0.0 collective-permute-done.15
  97.2 0.5 collective-permute-done.16
  97.8 1.1 pad_maximum_fusion
  98.8 13.5 %gather_fusion.1 = bf16[512,64,128]{2,1,0:T(8,128)(2,1)} fusion(bf16[36,64,128]{2,1,0:T(8,128)(2,1)S(1)} %bitcast.45, s32[1024]{0:T(1024)S(1)} %pad_clamp_fusion), kind=kCustom, calls=%fused_computation.1 | custom fusion | bytes 16779264 | tf_op jit(solution)/shard_map/gather | solution.py:45
  112.3 0.0 collective-permute-done.12
  112.3 7.0 %collective-permute-start.13 = (bf16[2048,128]{1,0:T(8,128)(2,1)}, bf16[2048,128]{1,0:T(8,128)(2,1)S(1)}, u32[]{:S(2)}, u32[]{:S(2)}) collective-permute-start(bf16[2048,128]{1,0:T(8,128)(2,1)} %collective-permute-done.12), channel_id=1, source_target_pairs={{1,0},{2,1},{3,2},{4,3},{5,4},{6,5},{7,6},{8,7},{9,8},{10,9},{11,1... | collective-permute-start | bytes 1572872 | tf_op jit(solution)/shard_map/ppermute | solution.py:56
  119.3 0.0 collective-permute-done.6
  119.3 1.9 collective-permute-start.7
  121.2 6.3 %convolution_convert_fusion = bf16[32,128,64]{1,2,0:T(8,128)(2,1)S(1)} fusion(bf16[32,64,1024]{2,1,0:T(8,128)(2,1)} %param.5, bf16[32,1024,128]{2,1,0:T(8,128)(2,1)} %bitcast.46), kind=kOutput, calls=%fused_computation.2 | convolution fusion | flops 537133056 | bytes 13107200 | tf_op jit(solution)/shard_map/bim,bmc->bic/dot_general | solution.py:46
  127.5 0.0 copy-start
  127.5 0.0 collective-permute-done.13
  127.5 7.4 %collective-permute-start.14 = (bf16[2048,128]{1,0:T(8,128)(2,1)S(1)}, bf16[2048,128]{1,0:T(8,128)(2,1)S(1)}, u32[]{:S(2)}, u32[]{:S(2)}) collective-permute-start(bf16[2048,128]{1,0:T(8,128)(2,1)S(1)} %collective-permute-done.13), channel_id=1, source_target_pairs={{1,0},{2,1},{3,2},{4,3},{5,4},{6,5},{7,6},{8,7},{9,8},{10,9},{11,1... | collective-permute-start | bytes 1572872 | tf_op jit(solution)/shard_map/ppermute | solution.py:56
  134.9 0.0 collective-permute-done.7
  134.9 0.8 bitcast_dynamic-update-slice_fusion.15
  135.8 1.9 bitcast_dynamic-update-slice_fusion.14
  137.6 1.9 bitcast_dynamic-update-slice_fusion.13
  139.5 1.9 bitcast_dynamic-update-slice_fusion.12
  141.4 0.8 bitcast_dynamic-update-slice_fusion.11
  142.2 0.8 bitcast_dynamic-update-slice_fusion.10
  143.0 0.8 bitcast_dynamic-update-slice_fusion.9
  143.8 0.8 bitcast_dynamic-update-slice_fusion.8
  144.7 0.8 bitcast_dynamic-update-slice_fusion.7
  145.5 0.8 bitcast_dynamic-update-slice_fusion.6
  146.3 0.8 bitcast_dynamic-update-slice_fusion.5
  147.2 0.9 bitcast_dynamic-update-slice_fusion.4
  148.0 1.9 bitcast_dynamic-update-slice_fusion.3
  149.9 1.9 bitcast_dynamic-update-slice_fusion.2
  151.8 0.8 bitcast_dynamic-update-slice_fusion.1
  152.6 0.0 collective-permute-done.14
  152.6 0.9 bitcast_dynamic-update-slice_fusion
  153.5 8.1 %gather_fusion = bf16[16,2048,128]{2,1,0:T(8,128)(2,1)} fusion(bf16[16,2048,128]{2,1,0:T(8,128)(2,1)} %bitcast_dynamic-update-slice_fusion, s32[1024]{0:T(1024)S(1)} %pad_clamp_fusion.1), kind=kCustom, calls=%fused_computation | custom fusion | bytes 16777280 | tf_op jit(solution)/shard_map/gather | solution.py:59
  161.6 12.4 %copy.5 = bf16[2048,16,128]{0,2,1:T(8,128)(2,1)} copy(bf16[2048,16,128]{2,0,1:T(8,128)(2,1)} %bitcast.47) | data formatting | bytes 16777216 | tf_op jit(solution)/shard_map/transpose | solution.py:11
  174.0 6.8 %fusion.3 = f32[2048,128]{1,0:T(8,128)} fusion(bf16[2048,2048]{0,1:T(8,128)(2,1)} %bitcast.48, bf16[2048,128]{1,0:T(8,128)(2,1)S(1)} %bitcast.49), kind=kOutput, calls=%fused_computation.30 | convolution fusion | flops 1073741824 | bytes 9961472 | tf_op jit(solution)/shard_map/dot_general | solution.py:30
  180.7 0.0 reduce-scatter.2.cloned.1.call-update
  180.8 124.1 %reduce-scatter.2.cloned.1.call-done = f32[64,128]{1,0:T(8,128)} async-done(((f32[2048,128]{1,0:T(8,128)}), f32[64,128]{1,0:T(8,128)}) %reduce-scatter.2.cloned.1.call-update) | async-done | bytes 32784 | tf_op jit(solution)/shard_map/reduce_scatter | solution.py:62
  (12 shorter events, 0.0 us)
Async XLA Ops:
  6.5 298.3 %reduce-scatter.2.cloned.1.call-start = ((), (), s32[]{:S(2)}) async-start(), calls=%async_computation.1 | async-start | bytes 1081344 | tf_op jit(solution)/shard_map/reduce_scatter | solution.py:62
  6.5 15.8 %collective-permute-start = (bf16[2048,128]{1,0:T(8,128)(2,1)}, bf16[2048,128]{1,0:T(8,128)(2,1)S(1)}, u32[]{:S(2)}, u32[]{:S(2)}) collective-permute-start(bf16[2048,128]{1,0:T(8,128)(2,1)} %param.3), channel_id=1, source_target_pairs={{0,1},{1,2},{2,3},{3,4},{4,5},{5,6},{6,7},{7,8},{8,9},{9,10},{10,1... | collective-permute-start | bytes 1572872 | tf_op jit(solution)/shard_map/ppermute | solution.py:54
  22.3 13.8 %collective-permute-start.1 = (bf16[2048,128]{1,0:T(8,128)(2,1)S(1)}, bf16[2048,128]{1,0:T(8,128)(2,1)S(1)}, u32[]{:S(2)}, u32[]{:S(2)}) collective-permute-start(bf16[2048,128]{1,0:T(8,128)(2,1)S(1)} %collective-permute-done), channel_id=1, source_target_pairs={{0,1},{1,2},{2,3},{3,4},{4,5},{5,6},{6,7},{7,8},{8,9},{9,10},{10,1... | collective-permute-start | bytes 1572872 | tf_op jit(solution)/shard_map/ppermute | solution.py:54
  25.7 14.7 %collective-permute-start.8 = (bf16[2048,128]{1,0:T(8,128)(2,1)}, bf16[2048,128]{1,0:T(8,128)(2,1)S(1)}, u32[]{:S(2)}, u32[]{:S(2)}) collective-permute-start(bf16[2048,128]{1,0:T(8,128)(2,1)} %param.3), channel_id=1, source_target_pairs={{1,0},{2,1},{3,2},{4,3},{5,4},{6,5},{7,6},{8,7},{9,8},{10,9},{11,1... | collective-permute-start | bytes 1572872 | tf_op jit(solution)/shard_map/ppermute | solution.py:56
  36.1 14.4 %collective-permute-start.2 = (bf16[2048,128]{1,0:T(8,128)(2,1)S(1)}, bf16[2048,128]{1,0:T(8,128)(2,1)S(1)}, u32[]{:S(2)}, u32[]{:S(2)}) collective-permute-start(bf16[2048,128]{1,0:T(8,128)(2,1)S(1)} %collective-permute-done.1), channel_id=1, source_target_pairs={{0,1},{1,2},{2,3},{3,4},{4,5},{5,6},{6,7},{7,8},{8,9},{9,10},{10,1... | collective-permute-start | bytes 1572872 | tf_op jit(solution)/shard_map/ppermute | solution.py:54
  40.4 15.0 %collective-permute-start.9 = (bf16[2048,128]{1,0:T(8,128)(2,1)S(1)}, bf16[2048,128]{1,0:T(8,128)(2,1)S(1)}, u32[]{:S(2)}, u32[]{:S(2)}) collective-permute-start(bf16[2048,128]{1,0:T(8,128)(2,1)S(1)} %collective-permute-done.8), channel_id=1, source_target_pairs={{1,0},{2,1},{3,2},{4,3},{5,4},{6,5},{7,6},{8,7},{9,8},{10,9},{11,1... | collective-permute-start | bytes 1572872 | tf_op jit(solution)/shard_map/ppermute | solution.py:56
  50.5 14.4 %collective-permute-start.3 = (bf16[2048,128]{1,0:T(8,128)(2,1)S(1)}, bf16[2048,128]{1,0:T(8,128)(2,1)S(1)}, u32[]{:S(2)}, u32[]{:S(2)}) collective-permute-start(bf16[2048,128]{1,0:T(8,128)(2,1)S(1)} %collective-permute-done.2), channel_id=1, source_target_pairs={{0,1},{1,2},{2,3},{3,4},{4,5},{5,6},{6,7},{7,8},{8,9},{9,10},{10,1... | collective-permute-start | bytes 1572872 | tf_op jit(solution)/shard_map/ppermute | solution.py:54
  55.4 14.7 %collective-permute-start.10 = (bf16[2048,128]{1,0:T(8,128)(2,1)S(1)}, bf16[2048,128]{1,0:T(8,128)(2,1)S(1)}, u32[]{:S(2)}, u32[]{:S(2)}) collective-permute-start(bf16[2048,128]{1,0:T(8,128)(2,1)S(1)} %collective-permute-done.9), channel_id=1, source_target_pairs={{1,0},{2,1},{3,2},{4,3},{5,4},{6,5},{7,6},{8,7},{9,8},{10,9},{11,1... | collective-permute-start | bytes 1572872 | tf_op jit(solution)/shard_map/ppermute | solution.py:56
  64.9 5.3 %copy-start.3 = (bf16[2048,128]{1,0:T(8,128)(2,1)}, bf16[2048,128]{1,0:T(8,128)(2,1)S(1)}, u32[]{:S(2)}) copy-start(bf16[2048,128]{1,0:T(8,128)(2,1)S(1)} %collective-permute-done.3) | copy-start | bytes 1572868
  64.9 15.3 %collective-permute-start.4 = (bf16[2048,128]{1,0:T(8,128)(2,1)S(1)}, bf16[2048,128]{1,0:T(8,128)(2,1)}, u32[]{:S(2)}, u32[]{:S(2)}) collective-permute-start(bf16[2048,128]{1,0:T(8,128)(2,1)S(1)} %collective-permute-done.3), channel_id=1, source_target_pairs={{0,1},{1,2},{2,3},{3,4},{4,5},{5,6},{6,7},{7,8},{8,9},{9,10},{10,1... | collective-permute-start | bytes 1572872 | tf_op jit(solution)/shard_map/ppermute | solution.py:54
  70.1 27.1 %copy-start.1 = (bf16[2048,128]{1,0:T(8,128)(2,1)}, bf16[2048,128]{1,0:T(8,128)(2,1)S(1)}, u32[]{:S(2)}) copy-start(bf16[2048,128]{1,0:T(8,128)(2,1)S(1)} %collective-permute-done.10) | copy-start | bytes 1572868
  70.1 16.9 %collective-permute-start.11 = (bf16[2048,128]{1,0:T(8,128)(2,1)S(1)}, bf16[2048,128]{1,0:T(8,128)(2,1)}, u32[]{:S(2)}, u32[]{:S(2)}) collective-permute-start(bf16[2048,128]{1,0:T(8,128)(2,1)S(1)} %collective-permute-done.10), channel_id=1, source_target_pairs={{1,0},{2,1},{3,2},{4,3},{5,4},{6,5},{7,6},{8,7},{9,8},{10,9},{11,1... | collective-permute-start | bytes 1572872 | tf_op jit(solution)/shard_map/ppermute | solution.py:56
  80.1 15.0 %collective-permute-start.5 = (bf16[2048,128]{1,0:T(8,128)(2,1)}, bf16[2048,128]{1,0:T(8,128)(2,1)}, u32[]{:S(2)}, u32[]{:S(2)}) collective-permute-start(bf16[2048,128]{1,0:T(8,128)(2,1)} %collective-permute-done.4), channel_id=1, source_target_pairs={{0,1},{1,2},{2,3},{3,4},{4,5},{5,6},{6,7},{7,8},{8,9},{9,10},{10,1... | collective-permute-start | bytes 1572872 | tf_op jit(solution)/shard_map/ppermute | solution.py:54
  83.7 13.5 %collective-permute-start.15 = (bf16[128,128]{1,0:T(8,128)(2,1)S(1)}, bf16[128,128]{1,0:T(8,128)(2,1)S(1)}, u32[]{:S(2)}, u32[]{:S(2)}) collective-permute-start(bf16[128,128]{1,0:T(8,128)(2,1)S(1)} %get-tuple-element.5), channel_id=1, source_target_pairs={{0,16},{16,32},{32,48},{48,64},{64,80},{80,96},{96,112},{112,128},... | collective-permute-start | bytes 98312 | tf_op jit(solution)/shard_map/ppermute | solution.py:21
  85.0 12.8 %collective-permute-start.16 = (bf16[128,128]{1,0:T(8,128)(2,1)S(1)}, bf16[128,128]{1,0:T(8,128)(2,1)S(1)}, u32[]{:S(2)}, u32[]{:S(2)}) collective-permute-start(bf16[128,128]{1,0:T(8,128)(2,1)S(1)} %get-tuple-element.6), channel_id=1, source_target_pairs={{16,0},{32,16},{48,32},{64,48},{80,64},{96,80},{112,96},{128,112},... | collective-permute-start | bytes 98312 | tf_op jit(solution)/shard_map/ppermute | solution.py:24
  87.0 25.3 %collective-permute-start.12 = (bf16[2048,128]{1,0:T(8,128)(2,1)}, bf16[2048,128]{1,0:T(8,128)(2,1)}, u32[]{:S(2)}, u32[]{:S(2)}) collective-permute-start(bf16[2048,128]{1,0:T(8,128)(2,1)} %collective-permute-done.11), channel_id=1, source_target_pairs={{1,0},{2,1},{3,2},{4,3},{5,4},{6,5},{7,6},{8,7},{9,8},{10,9},{11,1... | collective-permute-start | bytes 1572872 | tf_op jit(solution)/shard_map/ppermute | solution.py:56
  95.1 24.2 %collective-permute-start.6 = (bf16[2048,128]{1,0:T(8,128)(2,1)}, bf16[2048,128]{1,0:T(8,128)(2,1)}, u32[]{:S(2)}, u32[]{:S(2)}) collective-permute-start(bf16[2048,128]{1,0:T(8,128)(2,1)} %collective-permute-done.5), channel_id=1, source_target_pairs={{0,1},{1,2},{2,3},{3,4},{4,5},{5,6},{6,7},{7,8},{8,9},{9,10},{10,1... | collective-permute-start | bytes 1572872 | tf_op jit(solution)/shard_map/ppermute | solution.py:54
  112.3 15.2 %collective-permute-start.13 = (bf16[2048,128]{1,0:T(8,128)(2,1)}, bf16[2048,128]{1,0:T(8,128)(2,1)S(1)}, u32[]{:S(2)}, u32[]{:S(2)}) collective-permute-start(bf16[2048,128]{1,0:T(8,128)(2,1)} %collective-permute-done.12), channel_id=1, source_target_pairs={{1,0},{2,1},{3,2},{4,3},{5,4},{6,5},{7,6},{8,7},{9,8},{10,9},{11,1... | collective-permute-start | bytes 1572872 | tf_op jit(solution)/shard_map/ppermute | solution.py:56
  119.3 15.6 %collective-permute-start.7 = (bf16[2048,128]{1,0:T(8,128)(2,1)}, bf16[2048,128]{1,0:T(8,128)(2,1)S(1)}, u32[]{:S(2)}, u32[]{:S(2)}) collective-permute-start(bf16[2048,128]{1,0:T(8,128)(2,1)} %collective-permute-done.6), channel_id=1, source_target_pairs={{0,1},{1,2},{2,3},{3,4},{4,5},{5,6},{6,7},{7,8},{8,9},{9,10},{10,1... | collective-permute-start | bytes 1572872 | tf_op jit(solution)/shard_map/ppermute | solution.py:54
  121.2 20.2 %copy-start.4 = (bf16[2048,128]{1,0:T(8,128)(2,1)S(1)}, bf16[2048,128]{1,0:T(8,128)(2,1)}, u32[]{:S(2)}) copy-start(bf16[2048,128]{1,0:T(8,128)(2,1)} %copy-done.3) | copy-start | bytes 1572868
  127.5 17.2 %copy-start = (bf16[2048,128]{1,0:T(8,128)(2,1)S(1)}, bf16[2048,128]{1,0:T(8,128)(2,1)}, u32[]{:S(2)}) copy-start(bf16[2048,128]{1,0:T(8,128)(2,1)} %param.3) | copy-start | bytes 1572868
  127.5 19.7 %copy-start.2 = (bf16[2048,128]{1,0:T(8,128)(2,1)S(1)}, bf16[2048,128]{1,0:T(8,128)(2,1)}, u32[]{:S(2)}) copy-start(bf16[2048,128]{1,0:T(8,128)(2,1)} %copy-done.1) | copy-start | bytes 1572868
  127.5 25.0 %collective-permute-start.14 = (bf16[2048,128]{1,0:T(8,128)(2,1)S(1)}, bf16[2048,128]{1,0:T(8,128)(2,1)S(1)}, u32[]{:S(2)}, u32[]{:S(2)}) collective-permute-start(bf16[2048,128]{1,0:T(8,128)(2,1)S(1)} %collective-permute-done.13), channel_id=1, source_target_pairs={{1,0},{2,1},{3,2},{4,3},{5,4},{6,5},{7,6},{8,7},{9,8},{10,9},{11,1... | collective-permute-start | bytes 1572872 | tf_op jit(solution)/shard_map/ppermute | solution.py:56
Sparse Core Ops, SparseCore 0:
  180.9 123.8 reduce-scatter.1
